TPU v7x, 1024 devices: a whole 4x8x16 slice. The times are simulated.
1024 devices in a mesh: fsdp: 64 (over y, z_lo), tensor: 16 (over z_hi, x, core).
Axes of the slice: x: 4, y: 8, z: 16 (z_hi: 2, z_lo: 8; z = z_hi * 8 + z_lo), core: 2. Of those that a mesh axis runs over, the one named last changes fastest.
Arguments:
- tokens: bfloat16 [8192, 4096], P(('fsdp', 'tensor')), may hold values from -24 to 24
- weight: bfloat16 [4096, 14336], P('fsdp', 'tensor'), may hold values from -0.25 to 0.25
- tile_pick: int32 [32, 16], replicated, may hold values from -1 to 6
- cotangent: bfloat16 [8192, 14336], P('fsdp', 'tensor'), may hold values from -6 to 6
Outputs:
- activated: bfloat16 [8192, 14336], P('fsdp', 'tensor')
- token_grad: bfloat16 [8192, 4096], P(('fsdp', 'tensor'))
- weight_grad: float32 [4096, 14336], P('fsdp', 'tensor')
Inputs may be any that keep to these rules, and one draw needn't show every extreme that they name: tile_pick[r, g] is the kept tile among the 7 tiles of column group g in tile row r, or -1 when none of them is kept.
All inputs are finite; a program needn't handle non-finite values.
Results may differ from a plain program's by a relative error of at most 0.013.
Values may be sent and summed in bfloat16 or wider, within the bound.
A program may use at most 32 MiB of HBM per device.

v0:
```python
import jax
import jax.numpy as jnp
from jax import lax
from jax.sharding import PartitionSpec as P

TILE = 128
GROUP = 7


precise_mode = lax.Precision.HIGHEST


def per_device(tokens, weight, tile_pick, cotangent):
    local_rows, panel_cols = weight.shape
    tile_rows = tile_pick.shape[0]
    feat_width = tokens.shape[1]
    group_rows = cotangent.shape[0]
    slots = panel_cols // (TILE * GROUP)
    packed_cols = slots * TILE
    fsdp_pos = lax.axis_index("fsdp")
    tensor_pos = lax.axis_index("tensor")
    my_picks = lax.dynamic_slice_in_dim(tile_pick, tensor_pos * slots, slots, 1)
    onehot = (my_picks[:, :, None] == jnp.arange(GROUP, dtype=jnp.int32)[None, None, :]).astype(
        jnp.float32
    )
    onehot_half = onehot.astype(jnp.bfloat16)
    row_tile = (fsdp_pos * local_rows + jnp.arange(local_rows, dtype=jnp.int32)) // TILE
    row_match = (row_tile[:, None] == jnp.arange(tile_rows, dtype=jnp.int32)[None, :]).astype(
        jnp.float32
    )
    row_pick = jnp.einsum("rq,qsj->rsj", row_match, onehot, precision=precise_mode)
    local_packed = jnp.einsum(
        "rsjn,rsj->rsn",
        weight.reshape(local_rows, slots, GROUP, TILE),
        row_pick.astype(jnp.bfloat16),
        preferred_element_type=jnp.float32,
    )
    local_packed = local_packed.astype(jnp.bfloat16).reshape(local_rows, packed_cols)
    panel = lax.all_gather(local_packed, "fsdp", axis=0, tiled=True)
    panel_three = panel.reshape(tile_rows, TILE, packed_cols)
    gathered = lax.all_gather(tokens, "tensor", axis=0, tiled=True)
    length = gathered.shape[0]
    partial_value = jnp.einsum(
        "trk,rkm->trm",
        gathered.reshape(length, tile_rows, TILE),
        panel_three,
        preferred_element_type=jnp.float32,
    )
    spread = jnp.einsum(
        "trsn,rsj->tsjn",
        partial_value.reshape(length, tile_rows, slots, TILE),
        onehot,
        precision=precise_mode,
    )
    pre_act = spread.reshape(length, panel_cols)
    sigmoid_pre = jax.nn.sigmoid(pre_act)
    activated = (pre_act * sigmoid_pre).astype(jnp.bfloat16)
    dpre = (
        cotangent.astype(jnp.float32) * sigmoid_pre * (1.0 + pre_act * (1.0 - sigmoid_pre))
    ).astype(jnp.bfloat16)
    dpacked = jnp.einsum(
        "tsjn,rsj->trsn",
        dpre.reshape(group_rows, slots, GROUP, TILE),
        onehot_half,
        preferred_element_type=jnp.float32,
    )
    dpacked = dpacked.astype(jnp.bfloat16).reshape(group_rows, tile_rows, packed_cols)
    partial_value = jnp.einsum(
        "trm,rkm->trk", dpacked, panel_three, preferred_element_type=jnp.float32
    ).reshape(tokens.shape[0] * lax.axis_size("tensor"), feat_width)
    token_grad = lax.psum_scatter(
        lax.optimization_barrier(partial_value.astype(jnp.bfloat16))
        .astype(jnp.float32)
        .astype(jnp.bfloat16),
        "tensor",
        scatter_dimension=0,
        tiled=True,
    )
    tile_sums = jnp.einsum(
        "trk,trm->rkm",
        gathered.reshape(group_rows, tile_rows, TILE),
        dpacked,
        preferred_element_type=jnp.float32,
    )
    my_tiles = lax.psum_scatter(
        tile_sums.reshape(feat_width, packed_cols), "fsdp", scatter_dimension=0, tiled=True
    )
    weight_grad = (my_tiles.reshape(local_rows, slots, 1, TILE) * row_pick[:, :, :, None]).reshape(
        local_rows, panel_cols
    )
    return (activated, token_grad, weight_grad)


def solution(mesh):
    placed = (P(("fsdp", "tensor"), None), P("fsdp", "tensor"), P(), P("fsdp", "tensor"))
    return jax.shard_map(
        per_device,
        mesh=mesh,
        in_specs=placed,
        out_specs=(P("fsdp", "tensor"), P(("fsdp", "tensor"), None), P("fsdp", "tensor")),
        check_vma=False,
    )
```

profile of v0, /device:TPU:1, one launch (start us, length us, event | category | flops | bytes accessed | tf_op | source)
XLA Modules:
  0.0 1133.3 jit_solution(4880340593324952976)
XLA Ops:
  7.2 0.7 all-gather.5.cloned.1.call-update
  8.3 1.1 reshape.163
  9.4 0.2 fusion.25
  9.6 0.6 convert_element_type.79
  10.3 1.1 copy.14
  11.4 95.1 %all-gather.5.cloned.1.call-done = bf16[128,4096]{1,0:T(8,128)(2,1)} async-done(((bf16[8,4096]{1,0:T(8,128)(2,1)}), bf16[128,4096]{1,0:T(8,128)(2,1)}) %all-gather.5.cloned.1.call-update) | async-done | bytes 1048592 | tf_op jit(solution)/shard_map/all_gather | solution.py:41
  106.5 1.6 copy.12
  108.1 378.4 %all-gather.3.cloned.1.call-done = bf16[4096,128]{1,0:T(8,128)(2,1)} async-done(((bf16[64,128]{1,0:T(8,128)(2,1)}), bf16[4096,128]{1,0:T(8,128)(2,1)}) %all-gather.3.cloned.1.call-update) | async-done | bytes 1048592 | tf_op jit(solution)/shard_map/all_gather | solution.py:39
  486.4 3.1 fusion.26
  489.5 3.1 copy.23
  492.6 2.4 fusion.3
  495.0 0.2 copy.13
  495.2 0.2 fusion.15
  495.4 0.2 copy.15
  495.6 0.5 fusion.2
  496.1 2.1 fusion.6
  498.3 1.1 copy-done.1
  499.5 0.9 convolution_convert_fusion
  500.3 1.3 copy.17
  501.8 0.8 copy.20
  502.6 457.7 %reduce-scatter.5.cloned.1.call-done = f32[64,128]{1,0:T(8,128)} async-done(((f32[4096,128]{1,0:T(8,128)}), f32[64,128]{1,0:T(8,128)}) %reduce-scatter.5.cloned.1.call-update) | async-done | bytes 32784 | tf_op jit(solution)/shard_map/reduce_scatter | solution.py:85
  960.3 0.9 broadcast_multiply_fusion
  961.2 0.7 copy.30
  961.9 164.9 %reduce-scatter.3.cloned.1.call-done = bf16[8,4096]{1,0:T(8,128)(2,1)} async-done(((bf16[128,4096]{1,0:T(8,128)(2,1)}), bf16[8,4096]{1,0:T(8,128)(2,1)}) %reduce-scatter.3.cloned.1.call-update) | async-done | bytes 65552 | tf_op jit(solution)/shard_map/reduce_scatter | solution.py:71
  (16 shorter events, 0.7 us)
Async XLA Ops:
  7.2 0.8 copy-start
  7.2 99.3 %all-gather.5.cloned.1.call-start = ((), (), s32[]{:S(2)}) async-start(), calls=%async_computation.3 | async-start | bytes 1114112 | tf_op jit(solution)/shard_map/all_gather | solution.py:41
  7.9 478.5 %all-gather.3.cloned.1.call-start = ((), (), s32[]{:S(2)}) async-start(), calls=%async_computation.2 | async-start | bytes 1064960 | tf_op jit(solution)/shard_map/all_gather | solution.py:39
  10.2 950.1 %reduce-scatter.5.cloned.1.call-start = ((), (), s32[]{:S(2)}) async-start(), calls=%async_computation.5 | async-start | bytes 2129920 | tf_op jit(solution)/shard_map/reduce_scatter | solution.py:85
  498.2 1.2 copy-start.1
  498.3 628.5 %reduce-scatter.3.cloned.1.call-start = ((), (), s32[]{:S(2)}) async-start(), calls=%async_computation.4 | async-start | bytes 1114112 | tf_op jit(solution)/shard_map/reduce_scatter | solution.py:71
Sparse Core Ops, SparseCore 0:
  12.5 93.9 all-gather.4
  109.7 376.6 all-gather.2
  498.4 461.8 reduce-scatter.4
  967.6 159.1 reduce-scatter.2
where the time goes:
time: 1130 us
  waiting for transfers between devices  1100 us (97%)
  between operations  13.9 us (1%)
  local copies, waits for them, and re-layouts  11.6 us (1%)
    reduce_scatter x1, waiting for transfers between devices, per_device(): lax.psum_scatter(tile_sums.reshape(feat_width, packed_cols), 'fsdp', scat...  458 us
    all_gather x1, waiting for transfers between devices, per_device(): panel = lax.all_gather(local_packed, 'fsdp', axis=0, tiled=True)  378 us
    reduce_scatter x1, waiting for transfers between devices, per_device(): lax.psum_scatter(lax.optimization_barrier(partial_value.astype(jnp.bfloat...  165 us
    all_gather x1, waiting for transfers between devices, per_device(): gathered = lax.all_gather(tokens, 'tensor', axis=0, tiled=True)  95.1 us
  transfers between devices with their start and end apart: 4, of which 4 were waited for; matrix products, arithmetic and copies ran while one was open for 1% of the time, Pallas kernels for 0%

commit v1 on v0

v1 whole, which is shorter than its diff:
```python
import functools

import jax
import jax.numpy as jnp
from jax import lax
from jax.experimental import pallas as pl
from jax.experimental.pallas import tpu as pltpu
from jax.sharding import PartitionSpec as P

TILE = 128
GROUP = 7
BF = jnp.bfloat16
F32 = jnp.float32


def kernel(dims, tok_in, w_in, picks, cot_in, act_out, tg_out, wg_out,
           tok, panel, xbuf, acc, dpre, dpick, pf, pb, g1, sb, g2, rb, g3,
           vf, vb, h1, uf, ub, h2,
           t1_s, t1_r, t2_s, t2_r, t3_s, t3_r, w1_s, w1_r, w2_s, w2_r,
           g1_s, g1_r, g2_s, g2_r, g3_s, g3_r, h1_s, h1_r, h2_s, h2_r):
    Y, Z, H, X = dims
    C = 2
    rows = w_in.shape[0]
    D = tok_in.shape[1]
    quarter = D // 4
    tile_rows = D // TILE
    f = lax.axis_index("fsdp")
    t = lax.axis_index("tensor")
    y, z = f // Z, f % Z
    h, x, c = t // (X * C), (t // C) % X, t % C

    def dev(yy=None, zz=None, hh=None, xx=None, cc=None):
        yy = y if yy is None else yy
        zz = z if zz is None else zz
        hh = h if hh is None else hh
        xx = x if xx is None else xx
        cc = c if cc is None else cc
        return (yy * Z + zz, (hh * X + xx) * C + cc)

    peers = (
        [dev(yy=(y + d) % Y) for d in range(1, Y)]
        + [dev(zz=(z + d) % Z) for d in range(1, Z)]
        + [dev(xx=(x + d) % X) for d in range(1, X)]
        + [dev(hh=1 - h), dev(cc=1 - c)]
    )
    barrier = pltpu.get_barrier_semaphore()
    for p in peers:
        pl.semaphore_signal(barrier, inc=1, device_id=p, device_id_type=pl.DeviceIdType.MESH)

    def copy(src, dst, ss, rs, device):
        return pltpu.make_async_remote_copy(
            src_ref=src, dst_ref=dst, send_sem=ss, recv_sem=rs,
            device_id=device, device_id_type=pl.DeviceIdType.MESH)

    def chosen(p, j):
        return jnp.full((1, TILE), (p == j).astype(F32)).astype(BF)

    def piece(cc, xx, hh):
        return (cc * X + xx) * H + hh

    own = tok_in[...].astype(F32)
    own = jnp.concatenate([own[:, k * quarter:(k + 1) * quarter] for k in range(4)], axis=0)
    me = piece(c, x, h)
    tok[me] = own.astype(BF)
    my_pick = picks[(f * rows) // TILE, t]
    mine = jnp.zeros((rows, TILE), BF)
    for j in range(GROUP):
        mine += w_in[:, j * TILE:(j + 1) * TILE] * chosen(my_pick, j)
    panel[f] = mine

    pl.semaphore_wait(barrier, len(peers))

    sent = []

    def go(src, dst, ss, rs, device):
        op = copy(src, dst, ss, rs, device)
        op.start()
        sent.append(op)

    def arrived(dst, ss, rs):
        copy(dst, dst, ss, rs, dev(cc=1 - c)).wait_recv()

    go(tok.at[me], tok.at[me], t1_s.at[0], t1_r.at[0], dev(hh=1 - h))
    for d in range(1, Z):
        go(panel.at[f], panel.at[f], w1_s.at[d], w1_r.at[d], dev(zz=(z + d) % Z))
    for d in range(1, X):
        go(tok.at[me], tok.at[me], t2_s.at[0, d], t2_r.at[0, d], dev(xx=(x + d) % X))
    go(tok.at[me], tok.at[me], t3_s.at[0, 0], t3_r.at[0, 0], dev(cc=1 - c))
    for d in range(1, Z):
        arrived(panel.at[y * Z + (z - d + Z) % Z], w1_s.at[d], w1_r.at[d])
    for d in range(1, Y):
        go(panel.at[pl.ds(y * Z, Z)], panel.at[pl.ds(y * Z, Z)], w2_s.at[d], w2_r.at[d],
           dev(yy=(y + d) % Y))
    for d in range(1, X):
        src = piece(c, (x - d + X) % X, h)
        arrived(tok.at[src], t2_s.at[0, d], t2_r.at[0, d])
        go(tok.at[src], tok.at[src], t3_s.at[0, d], t3_r.at[0, d], dev(cc=1 - c))
    src = piece(c, x, 1 - h)
    arrived(tok.at[src], t1_s.at[0], t1_r.at[0])
    for d in range(1, X):
        go(tok.at[src], tok.at[src], t2_s.at[1, d], t2_r.at[1, d], dev(xx=(x + d) % X))
    go(tok.at[src], tok.at[src], t3_s.at[1, 0], t3_r.at[1, 0], dev(cc=1 - c))
    for d in range(1, X):
        src = piece(c, (x - d + X) % X, 1 - h)
        arrived(tok.at[src], t2_s.at[1, d], t2_r.at[1, d])
        go(tok.at[src], tok.at[src], t3_s.at[1, d], t3_r.at[1, d], dev(cc=1 - c))
    for k in range(2):
        for d in range(X):
            src = piece(1 - c, (x - d + X) % X, h if k == 0 else 1 - h)
            arrived(tok.at[src], t3_s.at[k, d], t3_r.at[k, d])

    def assemble(i, _):
        hh, xx = i // X, i % X
        a = tok[piece(0, xx, hh)].astype(F32)
        b = tok[piece(1, xx, hh)].astype(F32)
        at = pl.ds(pl.multiple_of(i * 16, 16), 16)
        for k in range(4):
            both = jnp.concatenate([a[k * 8:k * 8 + 8], b[k * 8:k * 8 + 8]], axis=0)
            xbuf[at, k * quarter:(k + 1) * quarter] = both.astype(BF)
        return 0

    lax.fori_loop(0, H * X, assemble, 0)

    for d in range(1, Y):
        arrived(panel.at[pl.ds((y - d + Y) % Y * Z, Z)], w2_s.at[d], w2_r.at[d])

    blocks = TILE // rows
    acc[...] = jnp.zeros_like(acc)

    def tile_of(r):
        return panel[pl.ds(r * blocks, blocks)].reshape(TILE, TILE)

    def forward(i, _):
        r = i * 2
        p0, p1 = picks[r, t], picks[r + 1, t]
        w0, w1 = tile_of(r), tile_of(r + 1)
        cols = []
        for j in range(GROUP):
            cols.append(jnp.concatenate([w0 * chosen(p0, j), w1 * chosen(p1, j)], axis=0))
        wide = jnp.concatenate(cols, axis=1)
        acc[...] += jnp.dot(xbuf[:, pl.ds(pl.multiple_of(i * 2 * TILE, 2 * TILE), 2 * TILE)], wide,
                            preferred_element_type=F32)
        return 0

    lax.fori_loop(0, tile_rows // 2, forward, 0)
    for j in range(GROUP):
        at = slice(j * TILE, (j + 1) * TILE)
        pre = acc[:, at]
        s = jax.nn.sigmoid(pre)
        act_out[:, at] = (pre * s).astype(BF)
        dpre[:, at] = (cot_in[:, at].astype(F32) * s * (1.0 + pre * (1.0 - s))).astype(BF)

    def pick(r, _):
        p = picks[r, t]
        total = jnp.zeros((dpre.shape[0], TILE), BF)
        for j in range(GROUP):
            total += dpre[:, j * TILE:(j + 1) * TILE] * chosen(p, j)
        dpick[:, pl.ds(pl.multiple_of(r * TILE, TILE), TILE)] = total
        return 0

    lax.fori_loop(0, tile_rows, pick, 0)

    def weight_part(r, _):
        at = pl.ds(pl.multiple_of(r * TILE, TILE), TILE)
        g = lax.dot_general(xbuf[:, at], dpick[:, at], (((0,), (0,)), ((), ())),
                            preferred_element_type=F32)
        g = g.reshape(blocks, rows, TILE)
        vf[pl.ds(r * blocks, blocks)] = g
        vb[pl.ds(r * blocks, blocks)] = g.astype(BF)
        return 0

    lax.fori_loop(0, tile_rows, weight_part, 0)
    for d in range(1, Y):
        go(vb.at[pl.ds((y + d) % Y * Z, Z)], h1.at[d], h1_s.at[d], h1_r.at[d], dev(yy=(y + d) % Y))

    def token_part(r, _):
        at = pl.ds(pl.multiple_of(r * TILE, TILE), TILE)
        pf[:, at] = lax.dot_general(dpick[:, at], tile_of(r), (((1,), (1,)), ((), ())),
                                    preferred_element_type=F32)
        return 0

    lax.fori_loop(0, tile_rows, token_part, 0)

    def row_piece(cc, xx, hh):
        at = pl.ds(pl.multiple_of(((hh * X + xx) * C + cc) * 8, 8), 8)
        return jnp.concatenate(
            [pf[at, k * quarter:(k + 1) * quarter] for k in range(4)], axis=0)

    def to_sibling(i, _):
        pb[i] = row_piece(1 - c, i // H, i % H).astype(BF)
        return 0

    lax.fori_loop(0, X * H, to_sibling, 0)
    go(pb, g1, g1_s.at[0], g1_r.at[0], dev(cc=1 - c))
    arrived(g1, g1_s.at[0], g1_r.at[0])

    def chip_sum(i, _):
        sb[i] = (row_piece(c, i // H, i % H) + g1[i].astype(F32)).astype(BF)
        return 0

    lax.fori_loop(0, X * H, chip_sum, 0)
    for d in range(1, X):
        to = (x + d) % X
        go(sb.at[pl.ds(to * H, H)], g2.at[d], g2_s.at[d], g2_r.at[d], dev(xx=to))
    for d in range(1, X):
        arrived(g2.at[d], g2_s.at[d], g2_r.at[d])

    def line_sum(hh):
        total = row_piece(c, x, hh) + g1[x * H + hh].astype(F32)
        for d in range(1, X):
            total += g2[d, hh].astype(F32)
        return total

    rb[...] = line_sum(1 - h).astype(BF)
    go(rb, g3, g3_s.at[0], g3_r.at[0], dev(hh=1 - h))

    for d in range(1, Y):
        arrived(h1.at[d], h1_s.at[d], h1_r.at[d])

    def y_sum(i, _):
        total = vf[y * Z + i]
        for d in range(1, Y):
            total += h1[d, i].astype(F32)
        uf[i] = total
        ub[i] = total.astype(BF)
        return 0

    lax.fori_loop(0, Z, y_sum, 0)
    for d in range(1, Z):
        to = (z + d) % Z
        go(ub.at[to], h2.at[d], h2_s.at[d], h2_r.at[d], dev(zz=to))

    arrived(g3, g3_s.at[0], g3_r.at[0])
    total = line_sum(h) + g3[...].astype(F32)
    for k in range(4):
        tg_out[:, k * quarter:(k + 1) * quarter] = total[k * 8:k * 8 + 8].astype(BF)

    for d in range(1, Z):
        arrived(h2.at[d], h2_s.at[d], h2_r.at[d])
    total = uf[z]
    for d in range(1, Z):
        total += h2[d].astype(F32)
    for j in range(GROUP):
        wg_out[:, j * TILE:(j + 1) * TILE] = total * (my_pick == j).astype(F32)
    for op in sent:
        op.wait_send()


def make(mesh, dims):
    Y, Z, H, X = dims
    C = 2

    def per_device(tokens, weight, tile_pick, cotangent):
        D = tokens.shape[1]
        rows, cols = weight.shape
        group_rows = cotangent.shape[0]
        q = D // 4
        n = Y * Z
        dma = pltpu.SemaphoreType.DMA
        vm = pltpu.VMEM
        scratch = [
            vm((C * X * H, 32, q), BF), vm((n, rows, TILE), BF), vm((group_rows, D), BF),
            vm((group_rows, cols), F32), vm((group_rows, cols), BF), vm((group_rows, D), BF),
            vm((group_rows, D), F32),
            vm((X * H, 32, q), BF), vm((X * H, 32, q), BF), vm((X * H, 32, q), BF),
            vm((X, H, 32, q), BF), vm((32, q), BF), vm((32, q), BF),
            vm((n, rows, TILE), F32), vm((n, rows, TILE), BF), vm((Y, Z, rows, TILE), BF),
            vm((Z, rows, TILE), F32), vm((Z, rows, TILE), BF), vm((Z, rows, TILE), BF),
            dma((1,)), dma((1,)), dma((2, X)), dma((2, X)), dma((2, X)), dma((2, X)),
            dma((Z,)), dma((Z,)), dma((Y,)), dma((Y,)),
            dma((1,)), dma((1,)), dma((X,)), dma((X,)), dma((1,)), dma((1,)),
            dma((Y,)), dma((Y,)), dma((Z,)), dma((Z,)),
        ]
        spec = pl.BlockSpec(memory_space=pltpu.VMEM)
        return pl.pallas_call(
            functools.partial(kernel, dims),
            out_shape=(
                jax.ShapeDtypeStruct((group_rows, cols), BF),
                jax.ShapeDtypeStruct(tokens.shape, BF),
                jax.ShapeDtypeStruct((rows, cols), F32),
            ),
            in_specs=[spec, spec, pl.BlockSpec(memory_space=pltpu.SMEM), spec],
            out_specs=(spec, spec, spec),
            scratch_shapes=scratch,
            compiler_params=pltpu.CompilerParams(
                collective_id=0, has_side_effects=True, vmem_limit_bytes=40 * 2**20),
        )(tokens, weight, tile_pick, cotangent)

    placed = (P(("fsdp", "tensor"), None), P("fsdp", "tensor"), P(), P("fsdp", "tensor"))
    return jax.shard_map(
        per_device,
        mesh=mesh,
        in_specs=placed,
        out_specs=(P("fsdp", "tensor"), P(("fsdp", "tensor"), None), P("fsdp", "tensor")),
        check_vma=False,
    )


def solution(mesh):
    return make(mesh, (8, 8, 2, 4))
```

time: 1130 us -> 113 us (0.10)
  the two profiles are of different devices: /device:TPU:1 before, /device:TPU:20 now
where the time goes in v1:
time: 113 us; the launch traced here: 112 us
  Pallas kernels  106 us (94%)
  local copies, waits for them, and re-layouts  5.45 us (5%)
    pallas_call x1, Pallas kernels, per_device(): pl.pallas_call(functools.partial(kernel, dims), out_shape=(jax.ShapeDtype...  106 us
    unnamed x10, local copies, waits for them, and re-layouts  5.45 us

profile of v1, /device:TPU:20, one launch (start us, length us, event | category | flops | bytes accessed | tf_op | source)
XLA Modules:
  0.0 112.4 jit_solution(7155141578147940307)
XLA Ops:
  0.6 0.8 copy.7.picks
  1.4 0.0 copy-start
  1.4 0.9 copy-done
  2.3 0.0 copy-start.1
  2.3 0.9 copy-done.1
  3.2 0.0 copy-start.2
  3.2 0.8 copy-done.2
  4.1 106.3 %shard_map.67 = (bf16[128,896]{1,0:T(8,128)(2,1)S(1)}, bf16[8,4096]{1,0:T(8,128)(2,1)S(1)}, f32[64,896]{1,0:T(8,128)S(1)}) custom-call(bf16[8,4096]{1,0:T(8,128)(2,1)S(1)} %copy-done.2, bf16[64,896]{1,0:T(8,128)(2,1)S(1)} %copy-done.1, s32[32,16]{1,0:T(8,128)S(1)} %copy.7.picks, bf16[128,896]{1,0:T(8,128)(2,1)S(1)} %copy-done), custom_call_target="tpu_custom_call" | custom-call | tf_op jit(solution)/shard_map/pallas_call | solution.py:275
  110.4 0.7 copy.11
  111.1 0.6 copy.12
  111.7 0.7 copy.13
Async XLA Ops:
  1.4 0.9 copy-start
  2.3 0.9 copy-start.1
  3.2 0.8 copy-start.2

commit v2 on v1

v2 whole, which is shorter than its diff:
```python
import functools

import jax
import jax.numpy as jnp
from jax import lax
from jax.experimental import pallas as pl
from jax.experimental.pallas import tpu as pltpu
from jax.sharding import PartitionSpec as P

TILE = 128
GROUP = 7
BF = jnp.bfloat16
F32 = jnp.float32


def pair_order(p, k, pairs):
    if pairs != 4:
        return (p + k) % pairs
    inner = (p // 2 + p % 2) % 2
    kk = k if k < 2 else (2 + inner if k == 2 else 3 - inner)
    return (p // 2 + kk // 2) % 2 * 2 + (p % 2 + kk % 2) % 2


def kernel(dims, tok_hbm, w_hbm, picks, cot_hbm, act_out, tg_out, wg_out,
           tok_in, w_in, cot_in, tok, panel, xbuf, xt, acc, dpre, dpick, pf, pb, g1, sb, g2,
           rb, g3, vf, vb, h1, uf, ub, h2, in_s,
           t1_s, t1_r, t2_s, t2_r, t3_s, t3_r, w1_s, w1_r, w2_s, w2_r,
           g1_s, g1_r, g2_s, g2_r, g3_s, g3_r, h1_s, h1_r, h2_s, h2_r):
    Y, Z, H, X = dims
    C = 2
    NP = Z // 2
    rows = w_in.shape[0]
    D = tok_in.shape[1]
    quarter = D // 4
    tile_rows = D // TILE
    f = lax.axis_index("fsdp")
    t = lax.axis_index("tensor")
    y, z = f // Z, f % Z
    h, x, c = t // (X * C), (t // C) % X, t % C
    pz = z // 2

    def dev(yy=None, zz=None, hh=None, xx=None, cc=None):
        yy = y if yy is None else yy
        zz = z if zz is None else zz
        hh = h if hh is None else hh
        xx = x if xx is None else xx
        cc = c if cc is None else cc
        return (yy * Z + zz, (hh * X + xx) * C + cc)

    sibling = dev(cc=1 - c)
    partner = dev(hh=1 - h)
    peers = (
        [dev(zz=(z + d) % Z) for d in range(1, Z)]
        + [partner]
        + [dev(yy=(y + d) % Y) for d in range(1, Y)]
        + [dev(xx=(x + d) % X) for d in range(1, X)]
        + [sibling]
    )
    barrier = pltpu.get_barrier_semaphore()
    for p in peers:
        pl.semaphore_signal(barrier, inc=1, device_id=p, device_id_type=pl.DeviceIdType.MESH)

    loads = [pltpu.make_async_copy(a, b, in_s.at[i]) for i, (a, b) in enumerate(
        ((w_hbm, w_in), (tok_hbm, tok_in), (cot_hbm, cot_in)))]
    for op in loads:
        op.start()

    def copy(src, dst, ss, rs, device):
        return pltpu.make_async_remote_copy(
            src_ref=src, dst_ref=dst, send_sem=ss, recv_sem=rs,
            device_id=device, device_id_type=pl.DeviceIdType.MESH)

    sent = []

    def go(src, dst, ss, rs, device):
        op = copy(src, dst, ss, rs, device)
        op.start()
        sent.append(op)

    def arrived(dst, ss, rs):
        copy(dst, dst, ss, rs, sibling).wait_recv()

    def chosen(p, j):
        return jnp.full((1, TILE), (p == j).astype(F32)).astype(BF)

    def lanes(r):
        return pl.ds(pl.multiple_of(r * TILE, TILE), TILE)

    def piece(cc, xx, hh):
        return (cc * X + xx) * H + hh

    my_pick = picks[(f * rows) // TILE, t]
    loads[0].wait()
    mine = jnp.zeros((rows, TILE), BF)
    for j in range(GROUP):
        mine += w_in[:, j * TILE:(j + 1) * TILE] * chosen(my_pick, j)
    panel[f] = mine
    loads[1].wait()
    own = tok_in[...].astype(F32)
    own = jnp.concatenate([own[:, k * quarter:(k + 1) * quarter] for k in range(4)], axis=0)
    me = piece(c, x, h)
    tok[me] = own.astype(BF)

    def pair(k):
        return pair_order(pz, k, NP)

    def z_peer(n):
        if n == 0:
            return z + 1 - 2 * (z % 2)
        return pair((n + 1) // 2) * 2 + (n + 1) % 2

    def z_peers_of(k):
        return [0] if k == 0 else [2 * k - 1, 2 * k]

    pl.semaphore_wait(barrier, len(peers))

    go(tok.at[me], tok.at[me], t1_s.at[0], t1_r.at[0], partner)
    for n in range(Z - 1):
        go(panel.at[f], panel.at[f], w1_s.at[n], w1_r.at[z], dev(zz=z_peer(n)))
    for d in range(1, X):
        go(tok.at[me], tok.at[me], t2_s.at[0, d], t2_r.at[0, d], dev(xx=(x + d) % X))
    go(tok.at[me], tok.at[me], t3_s.at[0, 0], t3_r.at[0, 0], sibling)

    def weights_on(k):
        for n in z_peers_of(k):
            zs = z_peer(n)
            arrived(panel.at[y * Z + zs], w1_s.at[n], w1_r.at[zs])
        src = panel.at[pl.ds(y * Z + pair(k) * 2, 2)]
        for d in range(1, Y):
            go(src, src, w2_s.at[k, d], w2_r.at[k, d], dev(yy=(y + d) % Y))

    def tokens_on(rel):
        for d in range(1, X):
            src = piece(c, (x - d + X) % X, h if rel == 0 else 1 - h)
            arrived(tok.at[src], t2_s.at[rel, d], t2_r.at[rel, d])
            go(tok.at[src], tok.at[src], t3_s.at[rel, d], t3_r.at[rel, d], sibling)

    weights_on(0)
    if NP > 1:
        weights_on(1)
    tokens_on(0)
    for k in range(2, NP - 1):
        weights_on(k)
    src = piece(c, x, 1 - h)
    arrived(tok.at[src], t1_s.at[0], t1_r.at[0])
    for d in range(1, X):
        go(tok.at[src], tok.at[src], t2_s.at[1, d], t2_r.at[1, d], dev(xx=(x + d) % X))
    go(tok.at[src], tok.at[src], t3_s.at[1, 0], t3_r.at[1, 0], sibling)
    if NP > 2:
        weights_on(NP - 1)
    tokens_on(1)
    for k in range(2):
        for d in range(X):
            src = piece(1 - c, (x - d + X) % X, h if k == 0 else 1 - h)
            arrived(tok.at[src], t3_s.at[k, d], t3_r.at[k, d])

    def assemble(i, _):
        hh, xx = i // X, i % X
        a = tok[piece(0, xx, hh)].astype(F32)
        b = tok[piece(1, xx, hh)].astype(F32)
        at = pl.ds(pl.multiple_of(i * 16, 16), 16)
        for k in range(4):
            both = jnp.concatenate([a[k * 8:k * 8 + 8], b[k * 8:k * 8 + 8]], axis=0)
            xbuf[at, k * quarter:(k + 1) * quarter] = both.astype(BF)
        return 0

    lax.fori_loop(0, H * X, assemble, 0, unroll=2)

    def transpose(r, _):
        xt[r] = xbuf[:, lanes(r)].T
        return 0

    lax.fori_loop(0, tile_rows, transpose, 0, unroll=4)

    def tile_of(r):
        return panel[pl.ds(r * 2, 2)].reshape(TILE, TILE)

    for k in range(NP):
        for d in range(1, Y):
            at = pl.ds((y - d + Y) % Y * Z + pair(k) * 2, 2)
            arrived(panel.at[at], w2_s.at[k, d], w2_r.at[k, d])
        left, wide = [], []
        for yy in range(Y):
            r = yy * NP + pair(k)
            p = picks[r, t]
            w = tile_of(r)
            left.append(xbuf[:, lanes(r)])
            wide.append(jnp.concatenate([w * chosen(p, j) for j in range(GROUP)], axis=1))
        part = jnp.dot(jnp.concatenate(left, axis=1), jnp.concatenate(wide, axis=0),
                       preferred_element_type=F32)
        if k == 0:
            acc[...] = part
        else:
            acc[...] += part
    loads[2].wait()
    for j in range(GROUP):
        at = slice(j * TILE, (j + 1) * TILE)
        pre = acc[:, at]
        s = jax.nn.sigmoid(pre)
        act_out[:, at] = (pre * s).astype(BF)
        dpre[:, at] = (cot_in[:, at].astype(F32) * s * (1.0 + pre * (1.0 - s))).astype(BF)

    def weight_part(k, yy):
        r = yy * NP + pair(k)
        p = picks[r, t]
        total = dpre[:, 0:TILE] * chosen(p, 0)
        for j in range(1, GROUP):
            total += dpre[:, j * TILE:(j + 1) * TILE] * chosen(p, j)
        dpick[:, lanes(r)] = total
        g = jnp.dot(xt[r], total, preferred_element_type=F32)
        vb[r] = g.astype(BF)
        vf[r] = g

    for k in reversed(range(NP)):
        for yy in range(Y):
            weight_part(k, yy)
        for d in range(1, Y):
            to = (y + d) % Y
            go(vb.at[to * NP + pair(k)], h1.at[k, d], h1_s.at[k, d], h1_r.at[k, d], dev(yy=to))

    def token_part(r, _):
        pf[:, lanes(r)] = lax.dot_general(dpick[:, lanes(r)], tile_of(r), (((1,), (1,)), ((), ())),
                                          preferred_element_type=F32)
        return 0

    lax.fori_loop(0, tile_rows, token_part, 0, unroll=min(8, tile_rows))

    def row_piece(cc, xx, hh):
        at = pl.ds(pl.multiple_of(((hh * X + xx) * C + cc) * 8, 8), 8)
        return jnp.concatenate(
            [pf[at, k * quarter:(k + 1) * quarter] for k in range(4)], axis=0)

    h_of = (1 - h, h)
    for rel in range(2):
        for xx in range(X):
            pb[rel, xx] = row_piece(1 - c, xx, h_of[rel]).astype(BF)
        go(pb.at[rel], g1.at[rel], g1_s.at[rel], g1_r.at[rel], sibling)
    for rel in range(2):
        arrived(g1.at[rel], g1_s.at[rel], g1_r.at[rel])
        for d in range(1, X):
            to = (x + d) % X
            sb[rel, d] = (row_piece(c, to, h_of[rel]) + g1[rel, to].astype(F32)).astype(BF)
            go(sb.at[rel, d], g2.at[rel, d], g2_s.at[rel, d], g2_r.at[rel, d], dev(xx=to))

    def line_sum(rel):
        total = row_piece(c, x, h_of[rel]) + g1[rel, x].astype(F32)
        for d in range(1, X):
            arrived(g2.at[rel, d], g2_s.at[rel, d], g2_r.at[rel, d])
            total += g2[rel, d].astype(F32)
        return total

    rb[...] = line_sum(0).astype(BF)
    go(rb, g3, g3_s.at[0], g3_r.at[0], partner)
    own_tokens = line_sum(1)

    for k in reversed(range(NP)):
        total = vf[y * NP + pair(k)]
        for d in range(1, Y):
            arrived(h1.at[k, d], h1_s.at[k, d], h1_r.at[k, d])
            total += h1[k, d].astype(F32)
        total = total.reshape(2, rows, TILE)
        ub[k] = total.astype(BF)
        if k == 0:
            uf[...] = total
        for n in z_peers_of(k):
            to = z_peer(n)
            go(ub.at[k, to % 2], h2.at[z], h2_s.at[n], h2_r.at[z], dev(zz=to))

    arrived(g3, g3_s.at[0], g3_r.at[0])
    total = own_tokens + g3[...].astype(F32)
    for k in range(4):
        tg_out[:, k * quarter:(k + 1) * quarter] = total[k * 8:k * 8 + 8].astype(BF)

    total = uf[z % 2]
    for n in reversed(range(Z - 1)):
        zs = z_peer(n)
        arrived(h2.at[zs], h2_s.at[n], h2_r.at[zs])
        total += h2[zs].astype(F32)
    for j in range(GROUP):
        wg_out[:, j * TILE:(j + 1) * TILE] = total * (my_pick == j).astype(F32)
    for op in sent:
        op.wait_send()


def make(mesh, dims):
    Y, Z, H, X = dims
    C = 2
    NP = Z // 2

    def per_device(tokens, weight, tile_pick, cotangent):
        D = tokens.shape[1]
        rows, cols = weight.shape
        group_rows = cotangent.shape[0]
        q = D // 4
        n = Y * Z
        tr = D // TILE
        dma = pltpu.SemaphoreType.DMA
        vm = pltpu.VMEM
        scratch = [
            vm(tokens.shape, BF), vm(weight.shape, BF), vm(cotangent.shape, BF),
            vm((C * X * H, 32, q), BF), vm((n, rows, TILE), BF), vm((group_rows, D), BF),
            vm((tr, TILE, group_rows), BF),
            vm((group_rows, cols), F32), vm((group_rows, cols), BF), vm((group_rows, D), BF),
            vm((group_rows, D), F32),
            vm((H, X, 32, q), BF), vm((H, X, 32, q), BF), vm((H, X, 32, q), BF),
            vm((H, X, 32, q), BF), vm((32, q), BF), vm((32, q), BF),
            vm((tr, TILE, TILE), F32), vm((tr, TILE, TILE), BF), vm((NP, Y, TILE, TILE), BF),
            vm((2, rows, TILE), F32), vm((NP, 2, rows, TILE), BF), vm((Z, rows, TILE), BF),
            dma((3,)),
            dma((1,)), dma((1,)), dma((2, X)), dma((2, X)), dma((2, X)), dma((2, X)),
            dma((Z,)), dma((Z,)), dma((NP, Y)), dma((NP, Y)),
            dma((2,)), dma((2,)), dma((2, X)), dma((2, X)), dma((1,)), dma((1,)),
            dma((NP, Y)), dma((NP, Y)), dma((Z,)), dma((Z,)),
        ]
        spec = pl.BlockSpec(memory_space=pltpu.VMEM)
        far = pl.BlockSpec(memory_space=pltpu.HBM)
        return pl.pallas_call(
            functools.partial(kernel, dims),
            out_shape=(
                jax.ShapeDtypeStruct((group_rows, cols), BF),
                jax.ShapeDtypeStruct(tokens.shape, BF),
                jax.ShapeDtypeStruct((rows, cols), F32),
            ),
            in_specs=[far, far, pl.BlockSpec(memory_space=pltpu.SMEM), far],
            out_specs=(spec, spec, spec),
            scratch_shapes=scratch,
            compiler_params=pltpu.CompilerParams(
                collective_id=0, has_side_effects=True, vmem_limit_bytes=40 * 2**20),
        )(tokens, weight, tile_pick, cotangent)

    placed = (P(("fsdp", "tensor"), None), P("fsdp", "tensor"), P(), P("fsdp", "tensor"))
    return jax.shard_map(
        per_device,
        mesh=mesh,
        in_specs=placed,
        out_specs=(P("fsdp", "tensor"), P(("fsdp", "tensor"), None), P("fsdp", "tensor")),
        check_vma=False,
    )


def solution(mesh):
    return make(mesh, (8, 8, 2, 4))
```

time: 113 us -> 92.4 us (0.82)
  the two profiles are of different devices: /device:TPU:20 before, /device:TPU:22 now
where the time goes in v2:
time: 92.4 us; the launch traced here: 92.2 us
  Pallas kernels  86.1 us (93%)
  local copies, waits for them, and re-layouts  5.45 us (6%)
    pallas_call x1, Pallas kernels, per_device(): pl.pallas_call(functools.partial(kernel, dims), out_shape=(jax.ShapeDtype...  86.1 us
    unnamed x10, local copies, waits for them, and re-layouts  5.45 us

profile of v2, /device:TPU:22, one launch (start us, length us, event | category | flops | bytes accessed | tf_op | source)
XLA Modules:
  0.0 92.2 jit_solution(7950661587286383161)
XLA Ops:
  0.6 0.8 copy.7.picks
  1.4 0.0 copy-start
  1.4 0.9 %copy-done = bf16[128,896]{1,0:T(8,128)(2,1)S(1)} copy-done((bf16[128,896]{1,0:T(8,128)(2,1)S(1)}, bf16[128,896]{1,0:T(8,128)(2,1)}, u32[]{:S(2)}) %copy-start) | copy-done | bytes 229400
  2.3 0.0 copy-start.1
  2.3 0.9 copy-done.1
  3.2 0.0 copy-start.2
  3.2 0.8 copy-done.2
  4.1 86.1 %shard_map.67 = (bf16[128,896]{1,0:T(8,128)(2,1)S(1)}, bf16[8,4096]{1,0:T(8,128)(2,1)S(1)}, f32[64,896]{1,0:T(8,128)S(1)}) custom-call(bf16[8,4096]{1,0:T(8,128)(2,1)S(1)} %copy-done.2, bf16[64,896]{1,0:T(8,128)(2,1)S(1)} %copy-done.1, s32[32,16]{1,0:T(8,128)S(1)} %copy.7.picks, bf16[128,896]{1,0:T(8,128)(2,1)S(1)} %copy-done), custom_call_target="tpu_custom_call" | custom-call | tf_op jit(solution)/shard_map/pallas_call | solution.py:317
  90.1 0.7 copy.11
  90.8 0.6 copy.12
  91.5 0.7 copy.13
Async XLA Ops:
  1.4 0.9 %copy-start = (bf16[128,896]{1,0:T(8,128)(2,1)S(1)}, bf16[128,896]{1,0:T(8,128)(2,1)}, u32[]{:S(2)}) copy-start(bf16[128,896]{1,0:T(8,128)(2,1)} %cot_hbm.1) | copy-start | bytes 688132
  2.3 0.9 copy-start.1
  3.2 0.8 copy-start.2

commit v3 on v2

--- a/solution.py
+++ b/solution.py
@@ -11,6 +11,7 @@
 GROUP = 7
 BF = jnp.bfloat16
 F32 = jnp.float32
+GRANT = 40 * 2**20
 
 
 def pair_order(p, k, pairs):
@@ -23,7 +24,7 @@
 
 def kernel(dims, tok_hbm, w_hbm, picks, cot_hbm, act_out, tg_out, wg_out,
            tok_in, w_in, cot_in, tok, panel, xbuf, xt, acc, dpre, dpick, pf, pb, g1, sb, g2,
-           rb, g3, vf, vb, h1, uf, ub, h2, in_s,
+           rb, g3, vf, hs, hr, uf, ub, h2, in_s,
            t1_s, t1_r, t2_s, t2_r, t3_s, t3_r, w1_s, w1_r, w2_s, w2_r,
            g1_s, g1_r, g2_s, g2_r, g3_s, g3_r, h1_s, h1_r, h2_s, h2_r):
     Y, Z, H, X = dims
@@ -49,10 +50,11 @@
 
     sibling = dev(cc=1 - c)
     partner = dev(hh=1 - h)
+    right, left = dev(yy=(y + 1) % Y), dev(yy=(y + Y - 1) % Y)
     peers = (
         [dev(zz=(z + d) % Z) for d in range(1, Z)]
         + [partner]
-        + [dev(yy=(y + d) % Y) for d in range(1, Y)]
+        + [right, left]
         + [dev(xx=(x + d) % X) for d in range(1, X)]
         + [sibling]
     )
@@ -89,7 +91,7 @@
     def piece(cc, xx, hh):
         return (cc * X + xx) * H + hh
 
-    my_pick = picks[(f * rows) // TILE, t]
+    my_pick = picks[t, (f * rows) // TILE]
     loads[0].wait()
     mine = jnp.zeros((rows, TILE), BF)
     for j in range(GROUP):
@@ -121,13 +123,31 @@
         go(tok.at[me], tok.at[me], t2_s.at[0, d], t2_r.at[0, d], dev(xx=(x + d) % X))
     go(tok.at[me], tok.at[me], t3_s.at[0, 0], t3_r.at[0, 0], sibling)
 
-    def weights_on(k):
+    def hops(k, way):
+        return Y // 2 if (k + way) % 2 == 0 else Y - 1 - Y // 2
+
+    def behind(way, n):
+        return (y - n + Y) % Y if way == 0 else (y + n) % Y
+
+    def weights_go(k, way, hop):
+        if hop < hops(k, way):
+            at = panel.at[pl.ds(behind(way, hop) * Z + pair(k) * 2, 2)]
+            go(at, at, w2_s.at[way, k, hop], w2_r.at[way, k, hop], left if way else right)
+
+    def weights_here(k, way, hop):
+        at = panel.at[pl.ds(behind(way, hop + 1) * Z + pair(k) * 2, 2)]
+        arrived(at, w2_s.at[way, k, hop], w2_r.at[way, k, hop])
+
+    def weights_start(k):
         for n in z_peers_of(k):
             zs = z_peer(n)
             arrived(panel.at[y * Z + zs], w1_s.at[n], w1_r.at[zs])
-        src = panel.at[pl.ds(y * Z + pair(k) * 2, 2)]
-        for d in range(1, Y):
-            go(src, src, w2_s.at[k, d], w2_r.at[k, d], dev(yy=(y + d) % Y))
+        for way in range(2):
+            weights_go(k, way, 0)
+
+    def weights_on(k, way, hop):
+        weights_here(k, way, hop)
+        weights_go(k, way, hop + 1)
 
     def tokens_on(rel):
         for d in range(1, X):
@@ -135,20 +155,22 @@
             arrived(tok.at[src], t2_s.at[rel, d], t2_r.at[rel, d])
             go(tok.at[src], tok.at[src], t3_s.at[rel, d], t3_r.at[rel, d], sibling)
 
-    weights_on(0)
-    if NP > 1:
-        weights_on(1)
-    tokens_on(0)
-    for k in range(2, NP - 1):
-        weights_on(k)
-    src = piece(c, x, 1 - h)
-    arrived(tok.at[src], t1_s.at[0], t1_r.at[0])
-    for d in range(1, X):
-        go(tok.at[src], tok.at[src], t2_s.at[1, d], t2_r.at[1, d], dev(xx=(x + d) % X))
-    go(tok.at[src], tok.at[src], t3_s.at[1, 0], t3_r.at[1, 0], sibling)
-    if NP > 2:
-        weights_on(NP - 1)
-    tokens_on(1)
+    def partner_on():
+        src = piece(c, x, 1 - h)
+        arrived(tok.at[src], t1_s.at[0], t1_r.at[0])
+        for d in range(1, X):
+            go(tok.at[src], tok.at[src], t2_s.at[1, d], t2_r.at[1, d], dev(xx=(x + d) % X))
+        go(tok.at[src], tok.at[src], t3_s.at[1, 0], t3_r.at[1, 0], sibling)
+
+    steps = [(4.0, 0, tokens_on, (0,)), (8.0, 1, partner_on, ()), (11.0, 2, tokens_on, (1,))]
+    for k in range(NP):
+        start = 6.5 if k == NP - 1 else 5.0
+        steps.append((start, 3 + k, weights_start, (k,)))
+        for way in range(2):
+            for hop in range(hops(k, way) - 1):
+                steps.append((start + 2.6 * (hop + 1), 3 + k, weights_on, (k, way, hop)))
+    for _, _, step, what in sorted(steps, key=lambda s: (s[0], s[1], s[3])):
+        step(*what)
     for k in range(2):
         for d in range(X):
             src = piece(1 - c, (x - d + X) % X, h if k == 0 else 1 - h)
@@ -176,17 +198,17 @@
         return panel[pl.ds(r * 2, 2)].reshape(TILE, TILE)
 
     for k in range(NP):
-        for d in range(1, Y):
-            at = pl.ds((y - d + Y) % Y * Z + pair(k) * 2, 2)
-            arrived(panel.at[at], w2_s.at[k, d], w2_r.at[k, d])
-        left, wide = [], []
+        for way in range(2):
+            if hops(k, way):
+                weights_here(k, way, hops(k, way) - 1)
+        across, wide = [], []
         for yy in range(Y):
             r = yy * NP + pair(k)
-            p = picks[r, t]
+            p = picks[t, r]
             w = tile_of(r)
-            left.append(xbuf[:, lanes(r)])
+            across.append(xbuf[:, lanes(r)])
             wide.append(jnp.concatenate([w * chosen(p, j) for j in range(GROUP)], axis=1))
-        part = jnp.dot(jnp.concatenate(left, axis=1), jnp.concatenate(wide, axis=0),
+        part = jnp.dot(jnp.concatenate(across, axis=1), jnp.concatenate(wide, axis=0),
                        preferred_element_type=F32)
         if k == 0:
             acc[...] = part
@@ -202,21 +224,39 @@
 
     def weight_part(k, yy):
         r = yy * NP + pair(k)
-        p = picks[r, t]
+        p = picks[t, r]
         total = dpre[:, 0:TILE] * chosen(p, 0)
         for j in range(1, GROUP):
             total += dpre[:, j * TILE:(j + 1) * TILE] * chosen(p, j)
         dpick[:, lanes(r)] = total
         g = jnp.dot(xt[r], total, preferred_element_type=F32)
-        vb[r] = g.astype(BF)
         vf[r] = g
+        return g
+
+    def sums_go(k, way, hop, value):
+        hs[way, k, hop] = value.astype(BF)
+        go(hs.at[way, k, hop], hr.at[way, k, hop], h1_s.at[way, k, hop], h1_r.at[way, k, hop],
+           left if way else right)
+
+    def sums_here(k, way, hop):
+        arrived(hr.at[way, k, hop], h1_s.at[way, k, hop], h1_r.at[way, k, hop])
+        return hr[way, k, hop].astype(F32)
+
+    def sums_on(k, hop):
+        for way in range(2):
+            if hop + 1 < hops(k, way):
+                to = behind(1 - way, hops(k, way) - 1 - hop)
+                sums_go(k, way, hop + 1, sums_here(k, way, hop) + vf[to * NP + pair(k)])
 
     for k in reversed(range(NP)):
-        for yy in range(Y):
-            weight_part(k, yy)
-        for d in range(1, Y):
-            to = (y + d) % Y
-            go(vb.at[to * NP + pair(k)], h1.at[k, d], h1_s.at[k, d], h1_r.at[k, d], dev(yy=to))
+        for way in range(2):
+            if hops(k, way):
+                sums_go(k, way, 0, weight_part(k, behind(1 - way, hops(k, way))))
+    for k in reversed(range(NP)):
+        done = {hops(k, 0) or Y, Y - hops(k, 1)}
+        for off in range(Y):
+            if (off or Y) not in done or off == 0:
+                weight_part(k, (y + off) % Y)
 
     def token_part(r, _):
         pf[:, lanes(r)] = lax.dot_general(dpick[:, lanes(r)], tile_of(r), (((1,), (1,)), ((), ())),
@@ -235,6 +275,8 @@
         for xx in range(X):
             pb[rel, xx] = row_piece(1 - c, xx, h_of[rel]).astype(BF)
         go(pb.at[rel], g1.at[rel], g1_s.at[rel], g1_r.at[rel], sibling)
+    for k in reversed(range(NP)):
+        sums_on(k, 0)
     for rel in range(2):
         arrived(g1.at[rel], g1_s.at[rel], g1_r.at[rel])
         for d in range(1, X):
@@ -249,15 +291,20 @@
             total += g2[rel, d].astype(F32)
         return total
 
+    for k in reversed(range(NP)):
+        sums_on(k, 1)
     rb[...] = line_sum(0).astype(BF)
     go(rb, g3, g3_s.at[0], g3_r.at[0], partner)
+    for hop in range(2, Y // 2):
+        for k in reversed(range(NP)):
+            sums_on(k, hop)
     own_tokens = line_sum(1)
 
     for k in reversed(range(NP)):
         total = vf[y * NP + pair(k)]
-        for d in range(1, Y):
-            arrived(h1.at[k, d], h1_s.at[k, d], h1_r.at[k, d])
-            total += h1[k, d].astype(F32)
+        for way in range(2):
+            if hops(k, way):
+                total += sums_here(k, way, hops(k, way) - 1)
         total = total.reshape(2, rows, TILE)
         ub[k] = total.astype(BF)
         if k == 0:
@@ -280,6 +327,15 @@
         wg_out[:, j * TILE:(j + 1) * TILE] = total * (my_pick == j).astype(F32)
     for op in sent:
         op.wait_send()
+
+
+def write_out(a, b, c, a_out, b_out, c_out, sems):
+    ops = [pltpu.make_async_copy(src, dst, sems.at[i])
+           for i, (src, dst) in enumerate(((a, a_out), (b, b_out), (c, c_out)))]
+    for op in ops:
+        op.start()
+    for op in ops:
+        op.wait()
 
 
 def make(mesh, dims):
@@ -304,17 +360,18 @@
             vm((group_rows, D), F32),
             vm((H, X, 32, q), BF), vm((H, X, 32, q), BF), vm((H, X, 32, q), BF),
             vm((H, X, 32, q), BF), vm((32, q), BF), vm((32, q), BF),
-            vm((tr, TILE, TILE), F32), vm((tr, TILE, TILE), BF), vm((NP, Y, TILE, TILE), BF),
+            vm((tr, TILE, TILE), F32), vm((2, NP, Y // 2, TILE, TILE), BF),
+            vm((2, NP, Y // 2, TILE, TILE), BF),
             vm((2, rows, TILE), F32), vm((NP, 2, rows, TILE), BF), vm((Z, rows, TILE), BF),
             dma((3,)),
             dma((1,)), dma((1,)), dma((2, X)), dma((2, X)), dma((2, X)), dma((2, X)),
-            dma((Z,)), dma((Z,)), dma((NP, Y)), dma((NP, Y)),
+            dma((Z,)), dma((Z,)), dma((2, NP, Y // 2)), dma((2, NP, Y // 2)),
             dma((2,)), dma((2,)), dma((2, X)), dma((2, X)), dma((1,)), dma((1,)),
-            dma((NP, Y)), dma((NP, Y)), dma((Z,)), dma((Z,)),
+            dma((2, NP, Y // 2)), dma((2, NP, Y // 2)), dma((Z,)), dma((Z,)),
         ]
         spec = pl.BlockSpec(memory_space=pltpu.VMEM)
         far = pl.BlockSpec(memory_space=pltpu.HBM)
-        return pl.pallas_call(
+        results = pl.pallas_call(
             functools.partial(kernel, dims),
             out_shape=(
                 jax.ShapeDtypeStruct((group_rows, cols), BF),
@@ -325,8 +382,16 @@
             out_specs=(spec, spec, spec),
             scratch_shapes=scratch,
             compiler_params=pltpu.CompilerParams(
-                collective_id=0, has_side_effects=True, vmem_limit_bytes=40 * 2**20),
-        )(tokens, weight, tile_pick, cotangent)
+                collective_id=0, has_side_effects=True, vmem_limit_bytes=GRANT),
+        )(tokens, weight, tile_pick.T, cotangent)
+        return pl.pallas_call(
+            write_out,
+            out_shape=tuple(jax.ShapeDtypeStruct(r.shape, r.dtype) for r in results),
+            in_specs=[far] * 3,
+            out_specs=(far,) * 3,
+            scratch_shapes=[dma((3,))],
+            compiler_params=pltpu.CompilerParams(vmem_limit_bytes=GRANT),
+        )(*results)
 
     placed = (P(("fsdp", "tensor"), None), P("fsdp", "tensor"), P(), P("fsdp", "tensor"))
     return jax.shard_map(

time: 92.4 us -> 83.5 us (0.904)
  the two profiles are of different devices: /device:TPU:22 before, /device:TPU:1 now
where the time goes in v3:
time: 83.5 us; the launch traced here: 83.2 us
  Pallas kernels  79.2 us (95%)
  local copies, waits for them, and re-layouts  3.36 us (4%)
    pallas_call x1, Pallas kernels, per_device(): pl.pallas_call(functools.partial(kernel, dims), out_shape=(jax.ShapeDtype...  78.3 us
    unnamed x8, local copies, waits for them, and re-layouts  3.36 us

profile of v3, /device:TPU:1, one launch (start us, length us, event | category | flops | bytes accessed | tf_op | source)
XLA Modules:
  0.0 83.2 jit_solution(2382641737179670467)
XLA Ops:
  0.6 0.0 copy-start
  0.6 0.9 %copy-done = bf16[128,896]{1,0:T(8,128)(2,1)S(1)} copy-done((bf16[128,896]{1,0:T(8,128)(2,1)S(1)}, bf16[128,896]{1,0:T(8,128)(2,1)}, u32[]{:S(2)}) %copy-start) | copy-done | bytes 229400
  1.6 0.0 copy-start.1
  1.6 0.9 %copy-done.1 = bf16[64,896]{1,0:T(8,128)(2,1)S(1)} copy-done((bf16[64,896]{1,0:T(8,128)(2,1)S(1)}, bf16[64,896]{1,0:T(8,128)(2,1)}, u32[]{:S(2)}) %copy-start.1) | copy-done | bytes 114712
  2.5 0.0 copy-start.2
  2.5 0.8 %copy-done.2 = bf16[8,4096]{1,0:T(8,128)(2,1)S(1)} copy-done((bf16[8,4096]{1,0:T(8,128)(2,1)S(1)}, bf16[8,4096]{1,0:T(8,128)(2,1)}, u32[]{:S(2)}) %copy-start.2) | copy-done | bytes 65560
  3.3 0.0 copy-start.3
  3.3 0.7 copy-done.3
  4.0 78.3 %shard_map.67 = (bf16[128,896]{1,0:T(8,128)(2,1)S(1)}, bf16[8,4096]{1,0:T(8,128)(2,1)S(1)}, f32[64,896]{1,0:T(8,128)S(1)}) custom-call(bf16[8,4096]{1,0:T(8,128)(2,1)S(1)} %copy-done.2, bf16[64,896]{1,0:T(8,128)(2,1)S(1)} %copy-done.1, s32[16,32]{1,0:T(8,128)S(1)} %bitcast.1, bf16[128,896]{1,0:T(8,128)(2,1)S(1)} %copy-done), custom_call_target="tpu_custom_call" | custom-call | tf_op jit(solution)/shard_map/pallas_call | solution.py:374
  82.4 0.8 shard_map.68
Async XLA Ops:
  0.6 0.9 %copy-start = (bf16[128,896]{1,0:T(8,128)(2,1)S(1)}, bf16[128,896]{1,0:T(8,128)(2,1)}, u32[]{:S(2)}) copy-start(bf16[128,896]{1,0:T(8,128)(2,1)} %cot_hbm.1) | copy-start | bytes 688132
  1.6 0.9 %copy-start.1 = (bf16[64,896]{1,0:T(8,128)(2,1)S(1)}, bf16[64,896]{1,0:T(8,128)(2,1)}, u32[]{:S(2)}) copy-start(bf16[64,896]{1,0:T(8,128)(2,1)} %w_hbm.1) | copy-start | bytes 344068
  2.5 0.8 %copy-start.2 = (bf16[8,4096]{1,0:T(8,128)(2,1)S(1)}, bf16[8,4096]{1,0:T(8,128)(2,1)}, u32[]{:S(2)}) copy-start(bf16[8,4096]{1,0:T(8,128)(2,1)} %tok_hbm.1) | copy-start | bytes 196612
  3.3 0.7 copy-start.3

commit v4 on v3

--- a/solution.py
+++ b/solution.py
@@ -11,7 +11,7 @@
 GROUP = 7
 BF = jnp.bfloat16
 F32 = jnp.float32
-GRANT = 40 * 2**20
+GRANT = 54 * 2**20
 
 
 def pair_order(p, k, pairs):
@@ -162,7 +162,7 @@
             go(tok.at[src], tok.at[src], t2_s.at[1, d], t2_r.at[1, d], dev(xx=(x + d) % X))
         go(tok.at[src], tok.at[src], t3_s.at[1, 0], t3_r.at[1, 0], sibling)
 
-    steps = [(4.0, 0, tokens_on, (0,)), (8.0, 1, partner_on, ()), (11.0, 2, tokens_on, (1,))]
+    steps = [(3.0, 0, tokens_on, (0,)), (4.9, 1, partner_on, ()), (7.0, 2, tokens_on, (1,))]
     for k in range(NP):
         start = 6.5 if k == NP - 1 else 5.0
         steps.append((start, 3 + k, weights_start, (k,)))
@@ -329,13 +329,17 @@
         op.wait_send()
 
 
-def write_out(a, b, c, a_out, b_out, c_out, sems):
-    ops = [pltpu.make_async_copy(src, dst, sems.at[i])
-           for i, (src, dst) in enumerate(((a, a_out), (b, b_out), (c, c_out)))]
+def write_out(a, b, c, a_out, b_out, c_out, a_on, b_on, c_on, sems):
+    way = ((a, a_on, a_out), (b, b_on, b_out), (c, c_on, c_out))
+    ops = [pltpu.make_async_copy(src, on, sems.at[i]) for i, (src, on, _) in enumerate(way)]
+    outs = [pltpu.make_async_copy(on, dst, sems.at[3 + i]) for i, (_, on, dst) in enumerate(way)]
     for op in ops:
         op.start()
-    for op in ops:
+    for op, out in zip(ops, outs):
         op.wait()
+        out.start()
+    for out in outs:
+        out.wait()
 
 
 def make(mesh, dims):
@@ -389,7 +393,7 @@
             out_shape=tuple(jax.ShapeDtypeStruct(r.shape, r.dtype) for r in results),
             in_specs=[far] * 3,
             out_specs=(far,) * 3,
-            scratch_shapes=[dma((3,))],
+            scratch_shapes=[vm(r.shape, r.dtype) for r in results] + [dma((6,))],
             compiler_params=pltpu.CompilerParams(vmem_limit_bytes=GRANT),
         )(*results)
 

time: 83.5 us -> 82.7 us (level)
  local copies, waits for them, and re-layouts: 3.36 us -> 0 us
  Pallas kernels: 79.2 us -> 81.1 us
    unnamed x8 -> x0, local copies, waits for them, and re-layouts: 3.36 us -> none
    pallas_call x1, Pallas kernels: 0.81 us -> 1.82 us  [per_device(): pl.pallas_call(write_out, out_shape=tuple((jax.ShapeDtypeStruct(r.shape,...]
    pallas_call x1, Pallas kernels: 78.3 us -> 79.3 us  [per_device(): pl.pallas_call(functools.partial(kernel, dims), out_shape=(jax.ShapeDtype...]
where the time goes in v4:
time: 82.7 us; the launch traced here: 81.8 us
  Pallas kernels  81.1 us (98%)
    pallas_call x1, Pallas kernels, per_device(): pl.pallas_call(functools.partial(kernel, dims), out_shape=(jax.ShapeDtype...  79.3 us
    pallas_call x1, Pallas kernels, per_device(): pl.pallas_call(write_out, out_shape=tuple((jax.ShapeDtypeStruct(r.shape,...  1.82 us

profile of v4, /device:TPU:1, one launch (start us, length us, event | category | flops | bytes accessed | tf_op | source)
XLA Modules:
  0.0 81.8 jit_solution(12515275192989272266)
XLA Ops:
  0.6 79.3 %shard_map.67 = (bf16[128,896]{1,0:T(8,128)(2,1)}, bf16[8,4096]{1,0:T(8,128)(2,1)}, f32[64,896]{1,0:T(8,128)}) custom-call(bf16[8,4096]{1,0:T(8,128)(2,1)} %tok_hbm.1, bf16[64,896]{1,0:T(8,128)(2,1)} %w_hbm.1, s32[16,32]{1,0:T(8,128)} %bitcast.1, bf16[128,896]{1,0:T(8,128)(2,1)} %cot_hbm.1), custom_call_target="tpu_custom_call" | custom-call | tf_op jit(solution)/shard_map/pallas_call | solution.py:378
  80.0 1.8 %shard_map.68 = (bf16[128,896]{1,0:T(8,128)(2,1)}, bf16[8,4096]{1,0:T(8,128)(2,1)}, f32[64,896]{1,0:T(8,128)}) custom-call(bf16[128,896]{1,0:T(8,128)(2,1)} %get-tuple-element.6.a, bf16[8,4096]{1,0:T(8,128)(2,1)} %get-tuple-element.7.b, f32[64,896]{1,0:T(8,128)} %get-tuple-element.8.c), custom_call_target="tpu_custom_call" | custom-call | tf_op jit(solution)/shard_map/pallas_call | solution.py:391

commit v5 on v4

--- a/solution.py
+++ b/solution.py
@@ -162,7 +162,7 @@
             go(tok.at[src], tok.at[src], t2_s.at[1, d], t2_r.at[1, d], dev(xx=(x + d) % X))
         go(tok.at[src], tok.at[src], t3_s.at[1, 0], t3_r.at[1, 0], sibling)
 
-    steps = [(3.0, 0, tokens_on, (0,)), (4.9, 1, partner_on, ()), (7.0, 2, tokens_on, (1,))]
+    steps = [(3.0, 0, tokens_on, (0,)), (4.9, 1, partner_on, ()), (8.0, 2, tokens_on, (1,))]
     for k in range(NP):
         start = 6.5 if k == NP - 1 else 5.0
         steps.append((start, 3 + k, weights_start, (k,)))

time: 82.7 us -> 82.7 us (level)
  no operation moved by 1% of the time
where the time goes in v5:
time: 82.7 us; the launch traced here: 81.7 us
  Pallas kernels  81 us (98%)
    pallas_call x1, Pallas kernels, per_device(): pl.pallas_call(functools.partial(kernel, dims), out_shape=(jax.ShapeDtype...  79.2 us
    pallas_call x1, Pallas kernels, per_device(): pl.pallas_call(write_out, out_shape=tuple((jax.ShapeDtypeStruct(r.shape,...  1.82 us

profile of v5, /device:TPU:1, one launch (start us, length us, event | category | flops | bytes accessed | tf_op | source)
XLA Modules:
  0.0 81.7 jit_solution(1136528731140923564)
XLA Ops:
  0.6 79.2 %shard_map.67 = (bf16[128,896]{1,0:T(8,128)(2,1)}, bf16[8,4096]{1,0:T(8,128)(2,1)}, f32[64,896]{1,0:T(8,128)}) custom-call(bf16[8,4096]{1,0:T(8,128)(2,1)} %tok_hbm.1, bf16[64,896]{1,0:T(8,128)(2,1)} %w_hbm.1, s32[16,32]{1,0:T(8,128)} %bitcast.1, bf16[128,896]{1,0:T(8,128)(2,1)} %cot_hbm.1), custom_call_target="tpu_custom_call" | custom-call | tf_op jit(solution)/shard_map/pallas_call | solution.py:378
  79.8 1.8 %shard_map.68 = (bf16[128,896]{1,0:T(8,128)(2,1)}, bf16[8,4096]{1,0:T(8,128)(2,1)}, f32[64,896]{1,0:T(8,128)}) custom-call(bf16[128,896]{1,0:T(8,128)(2,1)} %get-tuple-element.6.a, bf16[8,4096]{1,0:T(8,128)(2,1)} %get-tuple-element.7.b, f32[64,896]{1,0:T(8,128)} %get-tuple-element.8.c), custom_call_target="tpu_custom_call" | custom-call | tf_op jit(solution)/shard_map/pallas_call | solution.py:391
